TPU v7x, 32 devices: a whole 2x2x4 slice. The times are simulated.
32 devices in a mesh: dp: 4 (over y, core), row: 2 (over x), col: 4 (over z).
Axes of the slice: x: 2, y: 2, z: 4, core: 2. Of those that a mesh axis runs over, the one named last changes fastest.
Arguments:
- tokens: bfloat16 [1024, 6144], P(('dp', 'col'), 'row'), may hold values from -6 to 6
- cotangent: bfloat16 [1024, 6144], P(('dp', 'col'), 'row'), may hold values from -6 to 6
- pre_act: bfloat16 [1024, 12288], P('dp', 'col'), may hold values from -6 to 6
- weight_in: bfloat16 [6144, 12288], P('row', 'col'), may hold values from -0.078125 to 0.078125
- weight_out: bfloat16 [12288, 6144], P('col', 'row'), may hold values from -0.0546875 to 0.0546875
Outputs:
- grad_tokens: bfloat16 [1024, 6144], P(('dp', 'col'), 'row')
- grad_in: float32 [6144, 12288], P('row', ('col', 'dp'))
- grad_out: float32 [12288, 6144], P(('col', 'dp'), 'row')
All inputs are finite; a program needn't handle non-finite values.
Results may differ from a plain program's by a relative error of at most 0.023.
Values may be sent and summed in bfloat16 or wider, within the bound.
A program may use at most 192 MiB of HBM per device.

v0:
```python
import jax
import jax.numpy as jnp
from jax import lax
from jax.sharding import PartitionSpec as P


def gelu_value(a):
    return 0.5 * a * (1.0 + lax.erf(a * 0.7071067811865476))


def gelu_slope(a):
    return (
        0.5 * (1.0 + lax.erf(a * 0.7071067811865476))
        + a * jnp.exp(-0.5 * a * a) * 0.3989422804014327
    )


def shards(tokens, cotangent, pre_act, weight_in, weight_out):
    contract = (((1,), (1,)), ((), ()))
    lead = (((0,), (0,)), ((), ()))
    tok_all, cot_all = (
        lax.all_gather(tokens, "col", axis=0, tiled=True),
        lax.all_gather(cotangent, "col", axis=0, tiled=True),
    )
    replica = tok_all.shape[0]
    total_tokens = replica * lax.axis_size("dp")
    factor = float(total_tokens) ** (-0.5)
    pre_float = pre_act.astype(jnp.float32)
    summed = lax.psum(
        lax.dot_general(cot_all, weight_out, contract, preferred_element_type=jnp.float32).astype(
            jnp.bfloat16
        ),
        "row",
    ).astype(jnp.float32)
    grad_pre = (summed * gelu_slope(pre_float)).astype(jnp.bfloat16)
    grad_tokens = lax.psum_scatter(
        lax.dot_general(grad_pre, weight_in, contract, preferred_element_type=jnp.float32).astype(
            jnp.bfloat16
        ),
        "col",
        scatter_dimension=0,
        tiled=True,
    )
    hidden = gelu_value(pre_float).astype(jnp.bfloat16)
    first = lax.dot_general(tok_all, grad_pre, lead, preferred_element_type=jnp.float32) * factor
    second = lax.dot_general(hidden, cot_all, lead, preferred_element_type=jnp.float32) * factor
    grad_in, grad_out = (
        lax.psum_scatter(first.astype(jnp.bfloat16), "dp", scatter_dimension=1, tiled=True).astype(
            jnp.float32
        ),
        lax.psum_scatter(second.astype(jnp.bfloat16), "dp", scatter_dimension=0, tiled=True).astype(
            jnp.float32
        ),
    )
    return (grad_tokens, grad_in, grad_out)


def solution(mesh):
    in_specs = (
        P(("dp", "col"), "row"),
        P(("dp", "col"), "row"),
        P("dp", "col"),
        P("row", "col"),
        P("col", "row"),
    )
    out_specs = (P(("dp", "col"), "row"), P("row", ("col", "dp")), P(("col", "dp"), "row"))
    return jax.shard_map(shards, mesh=mesh, in_specs=in_specs, out_specs=out_specs, check_vma=False)
```

profile of v0, /device:TPU:0, one launch (start us, length us, event | category | flops | bytes accessed | tf_op | source)
XLA Modules:
  0.0 469.2 jit_solution(8932405080684482068)
XLA Ops:
  7.2 0.0 all-gather.3.cloned.1.call-start
  7.2 0.7 all-gather.3.cloned.1.call-update
  7.9 0.0 all-gather.5.cloned.1.call-start
  7.9 0.7 all-gather.5.cloned.1.call-update
  8.6 0.0 copy-start
  8.7 0.0 all-reduce.2.cloned.1.call-start
  8.7 40.7 %all-gather.3.cloned.1.call-done = bf16[256,3072]{1,0:T(8,128)(2,1)} async-done(((bf16[64,3072]{1,0:T(8,128)(2,1)}), bf16[256,3072]{1,0:T(8,128)(2,1)}) %all-gather.3.cloned.1.call-update) | async-done | bytes 1572880 | tf_op jit(solution)/shard_map/all_gather | solution.py:23
  49.4 0.0 copy-start.2
  49.4 12.7 %convolution_convert_fusion.1 = bf16[256,3072]{1,0:T(8,128)(2,1)} fusion(bf16[256,3072]{1,0:T(8,128)(2,1)} %all-gather.3.cloned.1.call-done, bf16[3072,3072]{1,0:T(8,128)(2,1)} %param.9), kind=kOutput, calls=%fused_computation.9 | convolution fusion | flops 4832624640 | bytes 22020096 | tf_op jit(solution)/shard_map/dot_general | solution.py:30
  62.1 0.0 all-reduce.2.cloned.1.call-update
  62.1 0.0 reduce-scatter.8.cloned.1.call-start
  62.1 0.0 copy-done
  62.1 0.0 copy-done.2
  62.2 9.3 %multiply_convert_fusion = bf16[3072,3072]{1,0:T(8,128)(2,1)} fusion(bf16[256,3072]{1,0:T(8,128)(2,1)S(1)} %copy-done.2, bf16[256,3072]{1,0:T(8,128)(2,1)S(1)} %copy-done), kind=kOutput, calls=%fused_computation | convolution fusion | flops 4855431168 | bytes 22020096 | tf_op jit(solution)/shard_map/dot_general | solution.py:46
  71.5 0.0 reduce-scatter.8.cloned.1.call-update
  71.5 0.0 reduce-scatter.6.cloned.1.call-start
  71.5 15.4 %all-gather.5.cloned.1.call-done = bf16[256,3072]{1,0:T(8,128)(2,1)} async-done(((bf16[64,3072]{1,0:T(8,128)(2,1)}), bf16[256,3072]{1,0:T(8,128)(2,1)}) %all-gather.5.cloned.1.call-update) | async-done | bytes 1572880 | tf_op jit(solution)/shard_map/all_gather | solution.py:22
  86.9 53.3 %all-reduce.2.cloned.1.call-done = bf16[256,3072]{1,0:T(8,128)(2,1)} async-done(((bf16[256,3072]{1,0:T(8,128)(2,1)}), bf16[256,3072]{1,0:T(8,128)(2,1)}) %all-reduce.2.cloned.1.call-update) | async-done | bytes 1572880 | tf_op jit(solution)/shard_map/psum | solution.py:29
  140.2 13.6 %fusion = bf16[3072,3072]{0,1:T(8,128)(2,1)} fusion(bf16[256,3072]{1,0:T(8,128)(2,1)} %all-gather.5.cloned.1.call-done, bf16[256,3072]{1,0:T(8,128)(2,1)S(1)} %copy-done, bf16[256,3072]{1,0:T(8,128)(2,1)} %all-reduce.2.cloned.1.call-done), kind=kOutput, calls=%fused_computation.2 | convolution fusion | flops 4860149760 | bytes 23592960 | tf_op jit(solution)/shard_map/dot_general | solution.py:45
  153.8 0.0 copy-start.1
  153.8 0.0 reduce-scatter.6.cloned.1.call-update
  153.8 0.0 reduce-scatter.4.cloned.1.call-start
  153.9 1.8 copy-done.1
  155.7 14.6 %convolution_convert_fusion = bf16[256,3072]{1,0:T(8,128)(2,1)} fusion(bf16[3072,3072]{1,0:T(8,128)(2,1)} %param.8, bf16[256,3072]{1,0:T(8,128)(2,1)S(1)} %copy-done, bf16[256,3072]{1,0:T(8,128)(2,1)S(1)} %copy-done.1), kind=kOutput, calls=%fused_computation.8 | convolution fusion | flops 4842061824 | bytes 23592960 | tf_op jit(solution)/shard_map/dot_general | solution.py:37
  170.3 0.0 reduce-scatter.4.cloned.1.call-update
  170.3 112.0 %reduce-scatter.8.cloned.1.call-done = bf16[768,3072]{1,0:T(8,128)(2,1)} async-done(((bf16[3072,3072]{1,0:T(8,128)(2,1)}), bf16[768,3072]{1,0:T(8,128)(2,1)}) %reduce-scatter.8.cloned.1.call-update) | async-done | bytes 4718608 | tf_op jit(solution)/shard_map/reduce_scatter | solution.py:51
  282.2 7.4 %convert_element_type.43 = f32[768,3072]{1,0:T(8,128)} convert(bf16[768,3072]{1,0:T(8,128)(2,1)} %reduce-scatter.8.cloned.1.call-done) | non-fusion elementwise | flops 2359296 | bytes 14155776 | tf_op jit(solution)/shard_map/convert_element_type | solution.py:51
  289.6 134.6 %reduce-scatter.6.cloned.1.call-done = bf16[3072,768]{0,1:T(8,128)(2,1)} async-done(((bf16[3072,3072]{0,1:T(8,128)(2,1)}), bf16[3072,768]{0,1:T(8,128)(2,1)}) %reduce-scatter.6.cloned.1.call-update) | async-done | bytes 4718608 | tf_op jit(solution)/shard_map/reduce_scatter | solution.py:48
  424.2 7.4 %copy.8 = f32[3072,768]{1,0:T(8,128)} copy(bf16[3072,768]{0,1:T(8,128)(2,1)} %reduce-scatter.6.cloned.1.call-done) | data formatting | bytes 14155776
  431.6 30.8 %reduce-scatter.4.cloned.1.call-done = bf16[64,3072]{1,0:T(8,128)(2,1)} async-done(((bf16[256,3072]{1,0:T(8,128)(2,1)}), bf16[64,3072]{1,0:T(8,128)(2,1)}) %reduce-scatter.4.cloned.1.call-update) | async-done | bytes 393232 | tf_op jit(solution)/shard_map/reduce_scatter | solution.py:36
Async XLA Ops:
  7.2 42.2 %all-gather.3.cloned.1.call-start = ((), (), s32[]{:S(2)}) async-start(), calls=%async_computation.3 | async-start | bytes 1966080 | tf_op jit(solution)/shard_map/all_gather | solution.py:23
  7.9 79.1 %all-gather.5.cloned.1.call-start = ((), (), s32[]{:S(2)}) async-start(), calls=%async_computation.6 | async-start | bytes 1966080 | tf_op jit(solution)/shard_map/all_gather | solution.py:22
  8.6 53.5 %copy-start = (bf16[256,3072]{1,0:T(8,128)(2,1)S(1)}, bf16[256,3072]{1,0:T(8,128)(2,1)}, u32[]{:S(2)}) copy-start(bf16[256,3072]{1,0:T(8,128)(2,1)} %param.7) | copy-start | bytes 4718596
  8.7 131.5 %all-reduce.2.cloned.1.call-start = ((), (), s32[]{:S(2)}) async-start(), calls=%async_computation.4 | async-start | bytes 3145728 | tf_op jit(solution)/shard_map/psum | solution.py:29
  49.4 12.8 %copy-start.2 = (bf16[256,3072]{1,0:T(8,128)(2,1)S(1)}, bf16[256,3072]{1,0:T(8,128)(2,1)}, u32[]{:S(2)}) copy-start(bf16[256,3072]{1,0:T(8,128)(2,1)} %all-gather.3.cloned.1.call-done) | copy-start | bytes 4718596
  62.1 220.2 %reduce-scatter.8.cloned.1.call-start = ((), (), s32[]{:S(2)}) async-start(), calls=%async_computation.8 | async-start | bytes 23592960 | tf_op jit(solution)/shard_map/reduce_scatter | solution.py:51
  71.5 352.7 %reduce-scatter.6.cloned.1.call-start = ((), (), s32[]{:S(2)}) async-start(), calls=%async_computation.7 | async-start | bytes 23592960 | tf_op jit(solution)/shard_map/reduce_scatter | solution.py:48
  153.8 1.9 copy-start.1
  153.8 308.5 %reduce-scatter.4.cloned.1.call-start = ((), (), s32[]{:S(2)}) async-start(), calls=%async_computation.5 | async-start | bytes 1966080 | tf_op jit(solution)/shard_map/reduce_scatter | solution.py:36
Sparse Core Ops, SparseCore 0:
  9.6 39.7 all-gather.2
  51.0 35.9 all-gather.4
  89.8 50.3 all-reduce.1
  142.8 139.3 reduce-scatter.7
  284.7 139.4 reduce-scatter.5
  427.0 35.2 reduce-scatter.3
where the time goes:
time: 470 us; the launch traced here: 469 us
  waiting for transfers between devices  388 us (83%)
  matrix products  50.2 us (11%)
  between operations  14.1 us (3%)
  local copies, waits for them, and re-layouts  9.18 us (2%)
  other arithmetic  7.37 us (2%)
    reduce_scatter x1, waiting for transfers between devices, shards(): lax.psum_scatter(first.astype(jnp.bfloat16), 'dp', scatter_dimension=1, t...  135 us
    reduce_scatter x1, waiting for transfers between devices, shards(): lax.psum_scatter(second.astype(jnp.bfloat16), 'dp', scatter_dimension=0,...  112 us
    psum x1, waiting for transfers between devices, shards(): lax.psum(lax.dot_general(cot_all, weight_out, contract, preferred_element...  53.3 us
    all_gather x1, waiting for transfers between devices, shards(): lax.all_gather(cotangent, 'col', axis=0, tiled=True)  40.7 us
    reduce_scatter x1, waiting for transfers between devices, shards(): lax.psum_scatter(lax.dot_general(grad_pre, weight_in, contract, preferred...  30.8 us
    all_gather x1, waiting for transfers between devices, shards(): lax.all_gather(tokens, 'col', axis=0, tiled=True)  15.4 us
    dot_general x1, matrix products, shards(): lax.dot_general(grad_pre, weight_in, contract, preferred_element_type=jnp...  14.6 us
    dot_general x1, matrix products, shards(): lax.dot_general(tok_all, grad_pre, lead, preferred_element_type=jnp.float32)  13.6 us
  transfers between devices with their start and end apart: 6, of which 6 were waited for; matrix products, arithmetic and copies ran while one was open for 14% of the time, Pallas kernels for 0%

commit v1 on v0

--- a/solution.py
+++ b/solution.py
@@ -2,6 +2,14 @@
 import jax.numpy as jnp
 from jax import lax
 from jax.sharding import PartitionSpec as P
+
+
+def compute_samples(u_in, axis_no):
+    u_in = jnp.moveaxis(u_in, 0, axis_no)
+    p_next = u_in.shape
+    return u_in.reshape(
+        *p_next[:axis_no], p_next[axis_no] * p_next[axis_no + 1], *p_next[axis_no + 2 :]
+    )
 
 
 def gelu_value(a):
@@ -18,9 +26,31 @@
 def shards(tokens, cotangent, pre_act, weight_in, weight_out):
     contract = (((1,), (1,)), ((), ()))
     lead = (((0,), (0,)), ((), ()))
+
+    def review_modes(block_here, along_axis, pos_dim):
+        n_dev_all = lax.axis_size(along_axis)
+        copies = [(num, (num + 1) % n_dev_all) for num in range(n_dev_all)]
+        newest, w_next = ([], [])
+        kk = 0
+        panels = [(pp, t) for t, pp in copies]
+        while kk < n_dev_all - 1:
+            if kk % 2 == 0:
+                newest.append(
+                    lax.ppermute(newest[-1] if newest else block_here, along_axis, copies)
+                )
+            else:
+                w_next.append(
+                    lax.ppermute(w_next[-1] if w_next else block_here, along_axis, panels)
+                )
+            kk = kk + 1
+        val = jnp.stack([*newest[::-1], block_here, *w_next])
+        outer = lax.axis_index(along_axis) - len(newest)
+        val = val[(jnp.arange(n_dev_all) - outer) % n_dev_all]
+        return compute_samples(val, pos_dim)
+
     tok_all, cot_all = (
         lax.all_gather(tokens, "col", axis=0, tiled=True),
-        lax.all_gather(cotangent, "col", axis=0, tiled=True),
+        review_modes(cotangent, "col", 0),
     )
     replica = tok_all.shape[0]
     total_tokens = replica * lax.axis_size("dp")

time: 470 us -> 433 us (0.921)
  waiting for transfers between devices: 388 us -> 345 us
  starting transfers between devices: 0.24 us -> 5.57 us
    all_gather x1 -> x0, waiting for transfers between devices: 40.7 us -> none  [shards(): lax.all_gather(cotangent, 'col', axis=0, tiled=True)]
    ppermute x0 -> x3, waiting for transfers between devices: none -> 26 us  [the longest x2 19 us: review_modes(): lax.ppermute(newest[-1] if newest else block_here, along_axis, copies)]
    psum x1, waiting for transfers between devices: 53.3 us -> 35.4 us  [shards(): lax.psum(lax.dot_general(cot_all, weight_out, contract, preferred_element...]
    all_gather x1, waiting for transfers between devices: 15.4 us -> 5.9 us  [shards(): lax.all_gather(tokens, 'col', axis=0, tiled=True)]
    ppermute x0 -> x3, starting transfers between devices: none -> 5.17 us  [the longest x2 3.08 us: review_modes(): lax.ppermute(newest[-1] if newest else block_here, along_axis, copies)]
  transfers between devices with their start and end apart: 6 -> 8, of which waited for: 6 -> 8; matrix products, arithmetic and copies ran while one was open for 14% -> 15% of each run, Pallas kernels for 0% -> 0%
where the time goes in v1:
time: 433 us; the launch traced here: 432 us
  waiting for transfers between devices  345 us (80%)
  matrix products  48.2 us (11%)
  between operations  15.7 us (4%)
  local copies, waits for them, and re-layouts  9.68 us (2%)
  other arithmetic  8.58 us (2%)
  starting transfers between devices  5.57 us (1%)
    reduce_scatter x1, waiting for transfers between devices, shards(): lax.psum_scatter(first.astype(jnp.bfloat16), 'dp', scatter_dimension=1, t...  134 us
    reduce_scatter x1, waiting for transfers between devices, shards(): lax.psum_scatter(second.astype(jnp.bfloat16), 'dp', scatter_dimension=0,...  112 us
    psum x1, waiting for transfers between devices, shards(): lax.psum(lax.dot_general(cot_all, weight_out, contract, preferred_element...  35.4 us
    reduce_scatter x1, waiting for transfers between devices, shards(): lax.psum_scatter(lax.dot_general(grad_pre, weight_in, contract, preferred...  30.9 us
    ppermute x2, waiting for transfers between devices, review_modes(): lax.ppermute(newest[-1] if newest else block_here, along_axis, copies)  19 us
    dot_general x1, matrix products, shards(): lax.dot_general(grad_pre, weight_in, contract, preferred_element_type=jnp...  14.7 us
    dot_general x1, matrix products, shards(): lax.dot_general(tok_all, grad_pre, lead, preferred_element_type=jnp.float32)  13.7 us
    dot_general x1, matrix products, shards(): lax.dot_general(cot_all, weight_out, contract, preferred_element_type=jnp...  10.5 us
  transfers between devices with their start and end apart: 8, of which 8 were waited for; matrix products, arithmetic and copies ran while one was open for 15% of the time, Pallas kernels for 0%

profile of v1, /device:TPU:0, one launch (start us, length us, event | category | flops | bytes accessed | tf_op | source)
XLA Modules:
  0.0 432.4 jit_solution(3788232171868378292)
XLA Ops:
  8.0 0.0 all-gather.2.cloned.1.call-start
  8.0 3.1 collective-permute-start
  11.1 2.1 collective-permute-start.2
  13.2 10.1 %collective-permute-done = bf16[64,3072]{1,0:T(8,128)(2,1)S(1)} collective-permute-done((bf16[64,3072]{1,0:T(8,128)(2,1)}, bf16[64,3072]{1,0:T(8,128)(2,1)S(1)}, u32[]{:S(2)}, u32[]{:S(2)}) %collective-permute-start) | collective-permute-done | bytes 393248 | tf_op jit(solution)/shard_map/ppermute | solution.py:39
  23.3 0.0 collective-permute-start.1
  23.3 0.0 all-gather.2.cloned.1.call-update
  23.4 0.0 all-reduce.2.cloned.1.call-start
  23.5 7.1 %collective-permute-done.2 = bf16[64,3072]{1,0:T(8,128)(2,1)S(1)} collective-permute-done((bf16[64,3072]{1,0:T(8,128)(2,1)}, bf16[64,3072]{1,0:T(8,128)(2,1)S(1)}, u32[]{:S(2)}, u32[]{:S(2)}) %collective-permute-start.2) | collective-permute-done | bytes 393248 | tf_op jit(solution)/shard_map/ppermute | solution.py:43
  30.5 8.8 %collective-permute-done.1 = bf16[64,3072]{1,0:T(8,128)(2,1)S(1)} collective-permute-done((bf16[64,3072]{1,0:T(8,128)(2,1)S(1)}, bf16[64,3072]{1,0:T(8,128)(2,1)S(1)}, u32[]{:S(2)}, u32[]{:S(2)}) %collective-permute-start.1) | collective-permute-done | bytes 393248 | tf_op jit(solution)/shard_map/ppermute | solution.py:39
  39.4 1.2 pad_maximum_fusion
  40.6 0.6 gather_fusion
  41.2 0.0 copy-start
  41.2 10.5 %convolution_convert_fusion.1 = bf16[256,3072]{1,0:T(8,128)(2,1)} fusion(bf16[256,3072]{1,0:T(8,128)(2,1)S(1)} %bitcast.14, bf16[3072,3072]{1,0:T(8,128)(2,1)} %param.9), kind=kOutput, calls=%fused_computation.10 | convolution fusion | flops 4832624640 | bytes 22020096 | tf_op jit(solution)/shard_map/dot_general | solution.py:60
  51.7 0.0 all-reduce.2.cloned.1.call-update
  51.8 0.0 reduce-scatter.8.cloned.1.call-start
  51.8 0.0 copy-done
  51.8 9.3 %multiply_convert_fusion = bf16[3072,3072]{1,0:T(8,128)(2,1)} fusion(bf16[256,3072]{1,0:T(8,128)(2,1)S(1)} %bitcast.15, bf16[256,3072]{1,0:T(8,128)(2,1)S(1)} %copy-done), kind=kOutput, calls=%fused_computation.1 | convolution fusion | flops 4855431168 | bytes 22020096 | tf_op jit(solution)/shard_map/dot_general | solution.py:76
  61.2 0.0 reduce-scatter.8.cloned.1.call-update
  61.2 0.0 reduce-scatter.6.cloned.1.call-start
  61.3 5.9 %all-gather.2.cloned.1.call-done = bf16[256,3072]{1,0:T(8,128)(2,1)} async-done(((bf16[64,3072]{1,0:T(8,128)(2,1)}), bf16[256,3072]{1,0:T(8,128)(2,1)}) %all-gather.2.cloned.1.call-update) | async-done | bytes 1572880 | tf_op jit(solution)/shard_map/all_gather | solution.py:52
  67.2 35.4 %all-reduce.2.cloned.1.call-done = bf16[256,3072]{1,0:T(8,128)(2,1)} async-done(((bf16[256,3072]{1,0:T(8,128)(2,1)}), bf16[256,3072]{1,0:T(8,128)(2,1)}) %all-reduce.2.cloned.1.call-update) | async-done | bytes 1572880 | tf_op jit(solution)/shard_map/psum | solution.py:59
  102.5 13.7 %fusion = bf16[3072,3072]{0,1:T(8,128)(2,1)} fusion(bf16[256,3072]{1,0:T(8,128)(2,1)} %all-gather.2.cloned.1.call-done, bf16[256,3072]{1,0:T(8,128)(2,1)S(1)} %copy-done, bf16[256,3072]{1,0:T(8,128)(2,1)} %all-reduce.2.cloned.1.call-done), kind=kOutput, calls=%fused_computation.3 | convolution fusion | flops 4860149760 | bytes 23592960 | tf_op jit(solution)/shard_map/dot_general | solution.py:75
  116.2 0.0 copy-start.1
  116.2 0.0 reduce-scatter.6.cloned.1.call-update
  116.2 0.2 reduce-scatter.4.cloned.1.call-start
  116.5 1.6 copy-done.1
  118.1 14.7 %convolution_convert_fusion = bf16[256,3072]{1,0:T(8,128)(2,1)} fusion(bf16[3072,3072]{1,0:T(8,128)(2,1)} %param.8, bf16[256,3072]{1,0:T(8,128)(2,1)S(1)} %copy-done, bf16[256,3072]{1,0:T(8,128)(2,1)S(1)} %copy-done.1), kind=kOutput, calls=%fused_computation.9 | convolution fusion | flops 4842061824 | bytes 23592960 | tf_op jit(solution)/shard_map/dot_general | solution.py:67
  132.8 0.0 reduce-scatter.4.cloned.1.call-update
  132.8 111.8 %reduce-scatter.8.cloned.1.call-done = bf16[768,3072]{1,0:T(8,128)(2,1)} async-done(((bf16[3072,3072]{1,0:T(8,128)(2,1)}), bf16[768,3072]{1,0:T(8,128)(2,1)}) %reduce-scatter.8.cloned.1.call-update) | async-done | bytes 4718608 | tf_op jit(solution)/shard_map/reduce_scatter | solution.py:81
  244.6 7.4 %convert_element_type.43 = f32[768,3072]{1,0:T(8,128)} convert(bf16[768,3072]{1,0:T(8,128)(2,1)} %reduce-scatter.8.cloned.1.call-done) | non-fusion elementwise | flops 2359296 | bytes 14155776 | tf_op jit(solution)/shard_map/convert_element_type | solution.py:81
  252.0 134.5 %reduce-scatter.6.cloned.1.call-done = bf16[3072,768]{0,1:T(8,128)(2,1)} async-done(((bf16[3072,3072]{0,1:T(8,128)(2,1)}), bf16[3072,768]{0,1:T(8,128)(2,1)}) %reduce-scatter.6.cloned.1.call-update) | async-done | bytes 4718608 | tf_op jit(solution)/shard_map/reduce_scatter | solution.py:78
  386.5 7.4 %copy.8 = f32[3072,768]{1,0:T(8,128)} copy(bf16[3072,768]{0,1:T(8,128)(2,1)} %reduce-scatter.6.cloned.1.call-done) | data formatting | bytes 14155776
  393.9 30.9 %reduce-scatter.4.cloned.1.call-done = bf16[64,3072]{1,0:T(8,128)(2,1)} async-done(((bf16[256,3072]{1,0:T(8,128)(2,1)}), bf16[64,3072]{1,0:T(8,128)(2,1)}) %reduce-scatter.4.cloned.1.call-update) | async-done | bytes 393232 | tf_op jit(solution)/shard_map/reduce_scatter | solution.py:66
  (2 shorter events, 0.0 us)
Async XLA Ops:
  8.0 59.2 %all-gather.2.cloned.1.call-start = ((), (), s32[]{:S(2)}) async-start(), calls=%async_computation.5 | async-start | bytes 1966080 | tf_op jit(solution)/shard_map/all_gather | solution.py:52
  8.0 15.3 %collective-permute-start = (bf16[64,3072]{1,0:T(8,128)(2,1)}, bf16[64,3072]{1,0:T(8,128)(2,1)S(1)}, u32[]{:S(2)}, u32[]{:S(2)}) collective-permute-start(bf16[64,3072]{1,0:T(8,128)(2,1)} %param.6), channel_id=1, source_target_pairs={{0,1},{1,2},{2,3},{3,0},{4,5},{5,6},{6,7},{7,4},{8,9},{9,10},{10,1... | collective-permute-start | bytes 1179656 | tf_op jit(solution)/shard_map/ppermute | solution.py:39
  11.1 19.4 %collective-permute-start.2 = (bf16[64,3072]{1,0:T(8,128)(2,1)}, bf16[64,3072]{1,0:T(8,128)(2,1)S(1)}, u32[]{:S(2)}, u32[]{:S(2)}) collective-permute-start(bf16[64,3072]{1,0:T(8,128)(2,1)} %param.6), channel_id=1, source_target_pairs={{1,0},{2,1},{3,2},{0,3},{5,4},{6,5},{7,6},{4,7},{9,8},{10,9},{11,1... | collective-permute-start | bytes 1179656 | tf_op jit(solution)/shard_map/ppermute | solution.py:43
  23.3 16.0 %collective-permute-start.1 = (bf16[64,3072]{1,0:T(8,128)(2,1)S(1)}, bf16[64,3072]{1,0:T(8,128)(2,1)S(1)}, u32[]{:S(2)}, u32[]{:S(2)}) collective-permute-start(bf16[64,3072]{1,0:T(8,128)(2,1)S(1)} %collective-permute-done), channel_id=1, source_target_pairs={{0,1},{1,2},{2,3},{3,0},{4,5},{5,6},{6,7},{7,4},{8,9},{9,10},{10,1... | collective-permute-start | bytes 1179656 | tf_op jit(solution)/shard_map/ppermute | solution.py:39
  23.4 79.2 %all-reduce.2.cloned.1.call-start = ((), (), s32[]{:S(2)}) async-start(), calls=%async_computation.3 | async-start | bytes 3145728 | tf_op jit(solution)/shard_map/psum | solution.py:59
  41.2 10.6 %copy-start = (bf16[256,3072]{1,0:T(8,128)(2,1)S(1)}, bf16[256,3072]{1,0:T(8,128)(2,1)}, u32[]{:S(2)}) copy-start(bf16[256,3072]{1,0:T(8,128)(2,1)} %param.7) | copy-start | bytes 4718596
  51.8 192.8 %reduce-scatter.8.cloned.1.call-start = ((), (), s32[]{:S(2)}) async-start(), calls=%async_computation.7 | async-start | bytes 23592960 | tf_op jit(solution)/shard_map/reduce_scatter | solution.py:81
  61.2 325.3 %reduce-scatter.6.cloned.1.call-start = ((), (), s32[]{:S(2)}) async-start(), calls=%async_computation.6 | async-start | bytes 23592960 | tf_op jit(solution)/shard_map/reduce_scatter | solution.py:78
  116.2 1.9 copy-start.1
  116.2 308.6 %reduce-scatter.4.cloned.1.call-start = ((), (), s32[]{:S(2)}) async-start(), calls=%async_computation.4 | async-start | bytes 1966080 | tf_op jit(solution)/shard_map/reduce_scatter | solution.py:66
Sparse Core Ops, SparseCore 0:
  23.5 43.6 all-gather.1
Sparse Core Ops, SparseCore 1:
  51.9 50.6 all-reduce.1
  105.2 139.4 reduce-scatter.7
  247.1 139.3 reduce-scatter.5
  389.5 35.3 reduce-scatter.3
